TPU v7x, 32 devices: a whole 2x2x4 slice. The times are simulated.
32 devices in a mesh: group: 2 (over x), layer: 8 (over z, y), latent: 2 (over core).
Axes of the slice: x: 2, y: 2, z: 4, core: 2. Of those that a mesh axis runs over, the one named last changes fastest.
Arguments:
- residual_in: bfloat16 [2, 2048, 1792], P(None, 'group'), parts along dimension 1, may hold values from -3 to 3
- mlp_target: bfloat16 [2, 2048, 1792], P(None, 'group'), parts along dimension 1, may hold values from -6 to 6
- enc_weight: bfloat16 [2, 1792, 8192], P(None, None, ('layer', 'latent')), may hold values from -0.046875 to 0.046875
- enc_bias: float32 [2, 8192], P(None, ('layer', 'latent')), may hold values from -1 to 1
- dec_weight: bfloat16 [3, 8192, 1792], P(None, ('layer', 'latent')), may hold values from -0.0625 to 0.0625
Outputs:
- grad_enc_weight: bfloat16 [4, 1792, 8192], P('group', None, ('layer', 'latent')), parts along dimension 0
- grad_enc_bias: float32 [4, 8192], P('group', ('layer', 'latent')), parts along dimension 0
- grad_dec_weight: bfloat16 [6, 8192, 1792], P('group', ('layer', 'latent')), parts along dimension 0
There are 2 independent parts, one for each index of `group`. A program takes and returns all parts, laid end to end along the dimension named above; an argument that names none is the same for every part. Nothing has to cross between parts.
All inputs are finite; a program needn't handle non-finite values.
Results may differ from a plain program's by a relative error of at most 0.0059.
Values may be sent and summed in bfloat16 or wider, within the bound.
A program may use at most 128 MiB of HBM per device.

v0:
```python
import jax
import jax.numpy as jnp
from jax import lax
from jax.sharding import PartitionSpec as P


def pair_index(source, target):
    return target * (target + 1) // 2 + source


def target_term(act_rows, dec_weight, target):
    total = jnp.dot(
        act_rows[0], dec_weight[pair_index(0, target)], preferred_element_type=jnp.float32
    )
    for source in range(1, target + 1):
        total = total + jnp.dot(
            act_rows[source],
            dec_weight[pair_index(source, target)],
            preferred_element_type=jnp.float32,
        )
    return total


def body(residual_in, mlp_target, enc_weight, enc_bias, dec_weight):
    layers = residual_in.shape[0]
    tokens = residual_in.shape[1]
    pre_act = (
        jnp.einsum("ltd,ldf->ltf", residual_in, enc_weight, preferred_element_type=jnp.float32)
        + enc_bias[:, None, :]
    )
    activity = jnp.maximum(pre_act, 0.0).astype(jnp.bfloat16)
    err_scale = float(tokens) ** (-0.5)
    partial_sums = jnp.stack(
        [target_term(activity, dec_weight, target) for target in range(layers)]
    )
    rebuilt = lax.psum(partial_sums, ("layer", "latent"))
    error_all = ((rebuilt - mlp_target.astype(jnp.float32)) * err_scale).astype(jnp.bfloat16)

    def error_of(target):
        return error_all[target]

    dec_grads = []
    for target in range(layers):
        error_target = error_of(target)
        for source in range(target + 1):
            block = jnp.einsum(
                "tf,td->fd", activity[source], error_target, preferred_element_type=jnp.float32
            )
            dec_grads.append(block.astype(jnp.bfloat16))
    grad_dec = jnp.stack(dec_grads)
    act_grads = []
    for source in range(layers):
        total = jnp.einsum(
            "td,fd->tf",
            error_of(source),
            dec_weight[pair_index(source, source)],
            preferred_element_type=jnp.float32,
        )
        for target in range(source + 1, layers):
            total = total + jnp.einsum(
                "td,fd->tf",
                error_of(target),
                dec_weight[pair_index(source, target)],
                preferred_element_type=jnp.float32,
            )
        act_grads.append(total)
    grad_act = jnp.stack(act_grads)
    grad_pre = jnp.where(pre_act > 0.0, grad_act, jnp.zeros_like(grad_act))
    grad_bias = jnp.sum(grad_pre, axis=1)
    grad_rounded = grad_pre.astype(jnp.bfloat16)
    grad_encoder = jnp.einsum(
        "ltd,ltf->ldf", residual_in, grad_rounded, preferred_element_type=jnp.float32
    ).astype(jnp.bfloat16)
    return (grad_encoder, grad_bias, grad_dec)


def solution(mesh):
    placed = (
        P(None, "group", None),
        P(None, "group", None),
        P(None, None, ("layer", "latent")),
        P(None, ("layer", "latent")),
        P(None, ("layer", "latent"), None),
    )
    return jax.shard_map(
        body,
        mesh=mesh,
        in_specs=placed,
        out_specs=(
            P("group", None, ("layer", "latent")),
            P("group", ("layer", "latent")),
            P("group", ("layer", "latent"), None),
        ),
        check_vma=False,
    )
```

profile of v0, /device:TPU:0, one launch (start us, length us, event | category | flops | bytes accessed | tf_op | source)
XLA Modules:
  0.0 357.9 jit_solution(3850194438537164052)
XLA Ops:
  7.2 0.0 all-reduce.2.cloned.1.call-start
  7.2 0.0 copy-start.2
  7.2 10.3 %maximum_convert_fusion = (bf16[2,1024,512]{2,1,0:T(8,128)(2,1)S(1)}, f32[2,1024,512]{2,1,0:T(8,128)}) fusion(f32[2,512]{1,0:T(2,128)} %param.8, bf16[2,1024,1792]{2,1,0:T(8,128)(2,1)} %param.5, bf16[2,1792,512]{2,1,0:T(8,128)(2,1)} %param.7), kind=kOutput, calls=%fused_computation.8 | convolution fusion | flops 3761242112 | bytes 17305600 | tf_op jit(solution)/shard_map/ltd,ldf->ltf/dot_general | solution.py:28
  17.5 0.0 copy-start
  17.5 0.0 copy-done.2
  17.5 2.1 fusion.17
  19.6 5.0 %convolution_bitcast_fusion = f32[1,1024,1792]{2,1,0:T(8,128)} fusion(bf16[3,512,1792]{2,1,0:T(8,128)(2,1)S(1)} %copy-done.2, bf16[2,1024,512]{2,1,0:T(8,128)(2,1)S(1)} %get-tuple-element.6), kind=kOutput, calls=%fused_computation.4 | convolution fusion | flops 1879048192 | bytes 10223616 | tf_op jit(solution)/shard_map/dot_general | solution.py:12
  24.6 0.0 copy-done
  24.6 5.0 %add_bitcast_fusion = f32[1,1024,1792]{2,1,0:T(8,128)} fusion(f32[1024,1792]{1,0:T(8,128)S(1)} %fusion.17, bf16[3,512,1792]{2,1,0:T(8,128)(2,1)S(1)} %copy-done.2, bf16[2,1024,512]{2,1,0:T(8,128)(2,1)S(1)} %get-tuple-element.6), kind=kOutput, calls=%fused_computation.2 | convolution fusion | flops 1880883200 | bytes 17563648 | tf_op jit(solution)/shard_map/dot_general | solution.py:16
  29.6 11.3 %pad_maximum_fusion = f32[2,1024,1792]{2,1,0:T(8,128)} fusion(f32[1,1024,1792]{2,1,0:T(8,128)} %add_bitcast_fusion, f32[1,1024,1792]{2,1,0:T(8,128)} %convolution_bitcast_fusion), kind=kLoop, calls=%fused_computation | loop fusion | flops 3670016 | bytes 29360128 | tf_op jit(solution)/shard_map/stack | solution.py:33
  40.9 0.0 copy-start.3
  41.0 0.0 all-reduce.2.cloned.1.call-update
  41.0 0.7 copy-done.3
  41.6 2.9 fusion.32
  44.5 264.8 %all-reduce.2.cloned.1.call-done = f32[2,1024,1792]{2,1,0:T(8,128)} async-done(((f32[2,1024,1792]{2,1,0:T(8,128)}), f32[2,1024,1792]{2,1,0:T(8,128)}) %all-reduce.2.cloned.1.call-update) | async-done | bytes 14680080 | tf_op jit(solution)/shard_map/psum | solution.py:36
  309.3 0.0 copy-start.1
  309.3 8.2 %multiply_convert_fusion = bf16[2,1024,1792]{2,1,0:T(8,128)(2,1)S(1)} fusion(f32[2,1024,1792]{2,1,0:T(8,128)} %all-reduce.2.cloned.1.call-done, bf16[2,1024,1792]{2,1,0:T(8,128)(2,1)} %param.6), kind=kLoop, calls=%fused_computation.1 | loop fusion | flops 14680064 | bytes 29360128 | tf_op jit(solution)/shard_map/convert_element_type | solution.py:37
  317.5 0.0 copy-done.1
  317.5 0.0 slice-start
  317.5 2.1 fusion.4
  319.6 0.0 slice-start.1
  319.6 3.3 fusion.5
  323.0 3.3 fusion.6
  326.3 0.0 slice-done
  326.3 0.0 slice-done.1
  326.3 2.1 fusion.21
  328.4 0.0 slice-start.2
  328.4 2.1 fusion.2
  330.5 0.0 slice-start.3
  330.5 2.1 add_bitcast_fusion.1
  332.6 1.3 fusion.7
  334.0 0.0 slice-done.2
  334.0 0.0 slice-done.3
  334.0 6.1 %fusion = bf16[2,1792,512]{1,2,0:T(8,128)(2,1)} fusion(bf16[2,1024,1792]{2,1,0:T(8,128)(2,1)S(1)} %bitcast.69, f32[1,1024,512]{2,1,0:T(8,128)S(1)} %fusion.21, f32[1,1024,512]{2,1,0:T(8,128)S(1)} %add_bitcast_fusion.1, u8[1024,512]{1,0:T(8,128)(4,1)S(1)} %fusion.32), kind=kOutput, calls=%fused_computation.12 | convolution fusion | flops 3769368576 | bytes 15728640 | tf_op jit(solution)/shard_map/ltd,ltf->ldf/dot_general | solution.py:71
  340.0 5.9 %copy.9 = bf16[2,1792,512]{2,1,0:T(8,128)(2,1)} copy(bf16[2,1792,512]{1,2,0:T(8,128)(2,1)} %fusion) | data formatting | bytes 7340032
  346.0 5.1 %pad_maximum_fusion.1 = bf16[3,512,1792]{2,1,0:T(8,128)(2,1)} fusion(bf16[1,512,1792]{2,1,0:T(8,128)(2,1)} %fusion.5, bf16[1,512,1792]{2,1,0:T(8,128)(2,1)S(1)} %fusion.4, bf16[1,512,1792]{2,1,0:T(8,128)(2,1)} %fusion.6), kind=kLoop, calls=%fused_computation.3 | loop fusion | flops 5505024 | bytes 11010048 | tf_op jit(solution)/shard_map/stack | solution.py:50
  (2 shorter events, 0.0 us)
Async XLA Ops:
  7.2 302.2 %all-reduce.2.cloned.1.call-start = ((), (), s32[]{:S(2)}) async-start(), calls=%async_computation | async-start | bytes 29360128 | tf_op jit(solution)/shard_map/psum | solution.py:36
  7.2 10.3 %copy-start.2 = (bf16[3,512,1792]{2,1,0:T(8,128)(2,1)S(1)}, bf16[3,512,1792]{2,1,0:T(8,128)(2,1)}, u32[]{:S(2)}) copy-start(bf16[3,512,1792]{2,1,0:T(8,128)(2,1)} %param.9) | copy-start | bytes 16515076
  17.5 7.1 %copy-start = (bf16[2,1024,512]{2,1,0:T(8,128)(2,1)}, bf16[2,1024,512]{2,1,0:T(8,128)(2,1)S(1)}, u32[]{:S(2)}) copy-start(bf16[2,1024,512]{2,1,0:T(8,128)(2,1)S(1)} %get-tuple-element.6) | copy-start | bytes 6291460
  40.9 0.7 copy-start.3
  309.3 8.2 %copy-start.1 = (bf16[2,1024,512]{2,1,0:T(8,128)(2,1)S(1)}, bf16[2,1024,512]{2,1,0:T(8,128)(2,1)}, u32[]{:S(2)}) copy-start(bf16[2,1024,512]{2,1,0:T(8,128)(2,1)} %copy-done) | copy-start | bytes 6291460
  317.5 8.8 %slice-start = ((s8[5505024]{0:T(1024)(128)(4,1)}), s8[4194304]{0:T(1024)(128)(4,1)S(1)}, s32[]{:S(2)}) async-start(s8[5505024]{0:T(1024)(128)(4,1)} %bitcast.66), calls=%async_computation.1 | async-start | bytes 8388608
  319.6 6.7 %slice-start.1 = ((s8[5505024]{0:T(1024)(128)(4,1)}), s8[1310720]{0:T(1024)(128)(4,1)S(1)}, s32[]{:S(2)}) async-start(s8[5505024]{0:T(1024)(128)(4,1)} %bitcast.66), calls=%async_computation.2 | async-start | bytes 2621440
  328.4 5.6 %slice-start.2 = ((s8[7340032]{0:T(1024)(128)(4,1)}), s8[4194304]{0:T(1024)(128)(4,1)S(1)}, s32[]{:S(2)}) async-start(s8[7340032]{0:T(1024)(128)(4,1)} %bitcast.68), calls=%async_computation.3 | async-start | bytes 8388608
  330.5 3.5 slice-start.3
Sparse Core Ops, SparseCore 0:
  41.1 268.1 all-reduce.1
where the time goes:
time: 358 us
  waiting for transfers between devices  265 us (74%)
  matrix products  43.5 us (12%)
  other arithmetic  28.8 us (8%)
  between operations  14.1 us (4%)
  local copies, waits for them, and re-layouts  6.65 us (2%)
    psum x1, waiting for transfers between devices, body(): rebuilt = lax.psum(partial_sums, ('layer', 'latent'))  265 us
    another operation x1, other arithmetic, body(): jnp.stack([target_term(activity, dec_weight, target) for target in range(...  11.3 us
    dot_general x1, matrix products, body(): jnp.einsum('ltd,ldf->ltf', residual_in, enc_weight, preferred_element_typ...  10.3 us
    dot_general x3, matrix products, body(): jnp.einsum('tf,td->fd', activity[source], error_target, preferred_element...  8.77 us
    convert_element_type x1, other arithmetic, body(): ((rebuilt - mlp_target.astype(jnp.float32)) * err_scale).astype(jnp.bfloa...  8.16 us
  transfers between devices with their start and end apart: 1, of which 1 were waited for; matrix products, arithmetic and copies ran while one was open for 1% of the time, Pallas kernels for 0%

commit v1 on v0

v1 whole, which is shorter than its diff:
```python
import functools

import jax
import jax.numpy as jnp
from jax import lax
from jax.experimental import pallas as pl
from jax.experimental.pallas import tpu as pltpu
from jax.sharding import PartitionSpec as P

MESH = pl.DeviceIdType.MESH


def pair_index(source, target):
    return target * (target + 1) // 2 + source


def ring_place(index, ring, folded):
    if not folded:
        return index
    side, along = index % 2, index // 2
    return (1 - side) * along + side * (ring - 1 - along)


def ring_index(place, ring, folded):
    if not folded:
        return place
    side = place // (ring // 2)
    return (1 - side) * (2 * place) + side * (2 * (ring - 1 - place) + 1)


def exchange_kernel(
    ring, folded, scale,
    act_ref, dec_ref, target_ref, err_ref,
    part, pair_send, pair_recv, run_send, run_recv, target_own,
    target_sem, pair_sems, run_sems, gather_sems, share_sems,
):
    layers, _, cores, rows, width = part.shape
    half = ring // 2
    core = lax.axis_index("latent")
    other = 1 - core
    me = ring_place(lax.axis_index("layer"), ring, folded)

    def place(distance):
        return (me + distance + ring) % ring

    neighbour = {step: {"layer": ring_index(place(step), ring, folded)} for step in (1, -1)}
    sibling = {"latent": other}

    target_load = pltpu.make_async_copy(
        target_ref.at[:, me, core], target_own, target_sem
    )
    target_load.start()

    barrier = pltpu.get_barrier_semaphore()
    for device in (neighbour[1], neighbour[-1], sibling):
        pl.semaphore_signal(barrier, inc=1, device_id=device, device_id_type=MESH)
    pl.semaphore_wait(barrier, 3)

    chains = [(0, 1, half), (1, -1, half), (0, -1, half - 1), (1, 1, half - 1)]

    def pair_copy(q):
        return pltpu.make_async_remote_copy(
            src_ref=pair_send.at[:, q], dst_ref=pair_recv.at[:, q],
            send_sem=pair_sems.at[0, q], recv_sem=pair_sems.at[1, q],
            device_id=sibling, device_id_type=MESH,
        )

    def run_copy(chain, step):
        return pltpu.make_async_remote_copy(
            src_ref=run_send.at[chain, step], dst_ref=run_recv.at[chain, step],
            send_sem=run_sems.at[0, chain, step], recv_sem=run_sems.at[1, chain, step],
            device_id=neighbour[chains[chain][1]], device_id_type=MESH,
        )

    def gather_copy(chain, step):
        layer, direction, _ = chains[chain]
        block = err_ref.at[layer, place(-direction * step), core]
        return pltpu.make_async_remote_copy(
            src_ref=block, dst_ref=block,
            send_sem=gather_sems.at[0, chain, step], recv_sem=gather_sems.at[1, chain, step],
            device_id=neighbour[direction], device_id_type=MESH,
        )

    def share_copy(layer, q, sender):
        block = err_ref.at[layer, q, sender]
        return pltpu.make_async_remote_copy(
            src_ref=block, dst_ref=block,
            send_sem=share_sems.at[0, layer, q], recv_sem=share_sems.at[1, layer, q],
            device_id=sibling, device_id_type=MESH,
        )

    def decode(order, carry):
        away = half - (order + 1) // 2
        q = place(away * (2 * (order % 2) - 1))
        start = pl.multiple_of(q * (cores * rows), cores * rows)
        for target in range(layers):
            total = jnp.dot(
                act_ref[0, pl.ds(start, cores * rows), :],
                dec_ref[pair_index(0, target)], preferred_element_type=jnp.float32,
            )
            for source in range(1, target + 1):
                total = total + jnp.dot(
                    act_ref[source, pl.ds(start, cores * rows), :],
                    dec_ref[pair_index(source, target)], preferred_element_type=jnp.float32,
                )
            for k in range(cores):
                part[target, q, k] = total[k * rows:(k + 1) * rows]
            pair_send[target, q] = part[target, q, other].astype(jnp.bfloat16)
        pair_copy(q).start()
        return carry

    def own_sum(layer, q):
        return part[layer, q, core] + pair_recv[layer, q].astype(jnp.float32)

    lax.fori_loop(0, 3, decode, 0)
    for step in range(half):
        for away in {0: (half, half - 1, 1 - half)}.get(
            step, (half - 1 - step, step + 1 - half) if step < half - 1 else (0,)
        ):
            pair_copy(place(away)).wait_recv()
        for chain, (layer, direction, hops) in enumerate(chains):
            if step >= hops:
                continue
            value = own_sum(layer, place(direction * (hops - step)))
            if step > 0:
                run_copy(chain, step - 1).wait_recv()
                value = value + run_recv[chain, step - 1].astype(jnp.float32)
            run_send[chain, step] = value.astype(jnp.bfloat16)
            run_copy(chain, step).start()
        if step == 0:
            lax.fori_loop(3, ring, decode, 0)

    target_load.wait()
    for layer in range(layers):
        value = own_sum(layer, me)
        for chain, (of, direction, hops) in sorted(
            enumerate(chains), key=lambda item: item[1][2]
        ):
            if of == layer:
                run_copy(chain, hops - 1).wait_recv()
                value = value + run_recv[chain, hops - 1].astype(jnp.float32)
        error = (value - target_own[layer].astype(jnp.float32)) * scale
        err_ref[layer, me, core] = error.astype(jnp.bfloat16)
        for chain, (of, direction, hops) in enumerate(chains):
            if of == layer:
                gather_copy(chain, 0).start()
        share_copy(layer, me, core).start()

    for step in range(half):
        for chain, (layer, direction, hops) in enumerate(chains):
            if step >= hops:
                continue
            gather_copy(chain, step).wait_recv()
            if step + 1 < hops:
                gather_copy(chain, step + 1).start()
            share_copy(layer, place(-direction * (step + 1)), core).start()

    for chain, (layer, direction, hops) in enumerate(chains):
        for step in range(hops):
            run_copy(chain, step).wait_send()
            gather_copy(chain, step).wait_send()

    def finish(q, carry):
        pair_copy(q).wait_send()
        for layer in range(layers):
            share_copy(layer, q, core).wait_send()
            share_copy(layer, q, other).wait_recv()
        return carry

    lax.fori_loop(0, ring, finish, 0)


def exchange(activity, dec_weight, mlp_target, ring, cores, scale):
    layers, tokens, width = mlp_target.shape
    rows = tokens // (ring * cores)
    half = ring // 2
    blocks = (layers, ring, cores, rows, width)
    err = pl.pallas_call(
        functools.partial(exchange_kernel, ring, ring == 8, scale),
        out_shape=jax.ShapeDtypeStruct(blocks, jnp.bfloat16),
        in_specs=[
            pl.BlockSpec(memory_space=pltpu.VMEM),
            pl.BlockSpec(memory_space=pltpu.VMEM),
            pl.BlockSpec(memory_space=pl.ANY),
        ],
        out_specs=pl.BlockSpec(memory_space=pltpu.VMEM),
        scratch_shapes=[
            pltpu.VMEM(blocks, jnp.float32),
            pltpu.VMEM((layers, ring, rows, width), jnp.bfloat16),
            pltpu.VMEM((layers, ring, rows, width), jnp.bfloat16),
            pltpu.VMEM((4, half, rows, width), jnp.bfloat16),
            pltpu.VMEM((4, half, rows, width), jnp.bfloat16),
            pltpu.VMEM((layers, rows, width), jnp.bfloat16),
            pltpu.SemaphoreType.DMA,
            pltpu.SemaphoreType.DMA((2, ring)),
            pltpu.SemaphoreType.DMA((2, 4, half)),
            pltpu.SemaphoreType.DMA((2, 4, half)),
            pltpu.SemaphoreType.DMA((2, layers, ring)),
        ],
        compiler_params=pltpu.CompilerParams(
            collective_id=0, has_side_effects=True, vmem_limit_bytes=56 * 1024 * 1024
        ),
        cost_estimate=pl.CostEstimate(
            flops=6 * tokens * width * activity.shape[2], bytes_accessed=2 ** 24, transcendentals=0
        ),
    )(activity, dec_weight, mlp_target.reshape(blocks))
    return err.reshape(layers, tokens, width)


def body(ring, cores, residual_in, mlp_target, enc_weight, enc_bias, dec_weight):
    layers = residual_in.shape[0]
    tokens = residual_in.shape[1]
    pre_act = (
        jnp.einsum("ltd,ldf->ltf", residual_in, enc_weight, preferred_element_type=jnp.float32)
        + enc_bias[:, None, :]
    )
    activity = jnp.maximum(pre_act, 0.0).astype(jnp.bfloat16)
    err_scale = float(tokens) ** (-0.5)
    error_all = exchange(activity, dec_weight, mlp_target, ring, cores, err_scale)

    dec_grads = []
    for target in range(layers):
        for source in range(target + 1):
            block = jnp.einsum(
                "tf,td->fd", activity[source], error_all[target], preferred_element_type=jnp.float32
            )
            dec_grads.append(block.astype(jnp.bfloat16))
    grad_dec = jnp.stack(dec_grads)
    act_grads = []
    for source in range(layers):
        total = jnp.einsum(
            "td,fd->tf",
            error_all[source],
            dec_weight[pair_index(source, source)],
            preferred_element_type=jnp.float32,
        )
        for target in range(source + 1, layers):
            total = total + jnp.einsum(
                "td,fd->tf",
                error_all[target],
                dec_weight[pair_index(source, target)],
                preferred_element_type=jnp.float32,
            )
        act_grads.append(total)
    grad_act = jnp.stack(act_grads)
    grad_pre = jnp.where(pre_act > 0.0, grad_act, jnp.zeros_like(grad_act))
    grad_bias = jnp.sum(grad_pre, axis=1)
    grad_rounded = grad_pre.astype(jnp.bfloat16)
    grad_encoder = jnp.einsum(
        "ltd,ltf->ldf", residual_in, grad_rounded, preferred_element_type=jnp.float32
    ).astype(jnp.bfloat16)
    return (grad_encoder, grad_bias, grad_dec)


def solution(mesh):
    placed = (
        P(None, "group", None),
        P(None, "group", None),
        P(None, None, ("layer", "latent")),
        P(None, ("layer", "latent")),
        P(None, ("layer", "latent"), None),
    )
    return jax.shard_map(
        functools.partial(body, mesh.shape["layer"], mesh.shape["latent"]),
        mesh=mesh,
        in_specs=placed,
        out_specs=(
            P("group", None, ("layer", "latent")),
            P("group", ("layer", "latent")),
            P("group", ("layer", "latent"), None),
        ),
        check_vma=False,
    )
```

time: 358 us -> 138 us (0.39)
  waiting for transfers between devices: 265 us -> 0 us
  Pallas kernels: 0 us -> 90.8 us
  other arithmetic: 28.8 us -> 5.09 us
  between operations: 14.1 us -> 0.72 us
  matrix products: 43.5 us -> 31.1 us
    psum x1 -> x0, waiting for transfers between devices: 265 us -> none  [body(): rebuilt = lax.psum(partial_sums, ('layer', 'latent'))]
    pallas_call x0 -> x1, Pallas kernels: none -> 90.8 us  [exchange(): pl.pallas_call(functools.partial(exchange_kernel, ring, ring == 8, scale)...]
    dot_general x9 -> x6, matrix products: 27.1 us -> 12.8 us  [the longest x3 6.56 us: body(): jnp.einsum('tf,td->fd', activity[source], error_all[target], preferred_el...]
    another operation x1 -> x0, other arithmetic: 11.3 us -> none  [body(): jnp.stack([target_term(activity, dec_weight, target) for target in range(...]
    convert_element_type x1 -> x0, other arithmetic: 8.16 us -> none  [body(): ((rebuilt - mlp_target.astype(jnp.float32)) * err_scale).astype(jnp.bfloa...]
    slice x0 -> x1, local copies, waits for them, and re-layouts: none -> 3.76 us  [body(): error_all[source]]
  transfers between devices with their start and end apart: 1 -> 0, of which waited for: 1 -> 0; matrix products, arithmetic and copies ran while one was open for 1% -> 0% of each run, Pallas kernels for 0% -> 0%
where the time goes in v1:
time: 138 us; the launch traced here: 137 us
  Pallas kernels  90.8 us (66%)
  matrix products  31.1 us (23%)
  local copies, waits for them, and re-layouts  9.73 us (7%)
  other arithmetic  5.09 us (4%)
    pallas_call x1, Pallas kernels, exchange(): pl.pallas_call(functools.partial(exchange_kernel, ring, ring == 8, scale)...  90.8 us
    dot_general x1, matrix products, body(): jnp.einsum('ltd,ldf->ltf', residual_in, enc_weight, preferred_element_typ...  9.5 us
    dot_general x1, matrix products, body(): jnp.einsum('ltd,ltf->ldf', residual_in, grad_rounded, preferred_element_t...  8.77 us
    dot_general x3, matrix products, body(): jnp.einsum('tf,td->fd', activity[source], error_all[target], preferred_el...  6.56 us
    unnamed x9, local copies, waits for them, and re-layouts  5.97 us
    dot_general x2, matrix products, body(): jnp.einsum('td,fd->tf', error_all[source], dec_weight[pair_index(source,...  4.17 us
    slice x1, local copies, waits for them, and re-layouts, body(): error_all[source]  3.76 us
    another operation x1, other arithmetic, body(): grad_dec = jnp.stack(dec_grads)  3.04 us

profile of v1, /device:TPU:0, one launch (start us, length us, event | category | flops | bytes accessed | tf_op | source)
XLA Modules:
  0.0 137.5 jit_solution(10774611420216040490)
XLA Ops:
  0.6 0.0 copy-start.1
  0.6 9.5 %maximum_convert_fusion = (bf16[2,1024,512]{2,1,0:T(8,128)(2,1)}, f32[2,1024,512]{2,1,0:T(8,128)S(1)}) fusion(f32[2,512]{1,0:T(2,128)} %param.8, bf16[2,1024,1792]{2,1,0:T(8,128)(2,1)} %param.5, bf16[2,1792,512]{2,1,0:T(8,128)(2,1)} %param.7), kind=kOutput, calls=%fused_computation.4 | convolution fusion | flops 3761242112 | bytes 17305600 | tf_op jit(solution)/shard_map/ltd,ldf->ltf/dot_general | solution.py:214
  10.1 0.0 copy-done.1
  10.1 0.7 fusion.23
  10.9 90.8 %shard_map.76 = bf16[2,8,2,64,1792]{4,3,2,1,0:T(8,128)(2,1)} custom-call(bf16[2,1024,512]{2,1,0:T(8,128)(2,1)} %get-tuple-element.8.act_ref, bf16[3,512,1792]{2,1,0:T(8,128)(2,1)} %dec_ref.1, bf16[2,8,2,64,1792]{4,3,2,1,0:T(8,128)(2,1)} %bitcast.44), custom_call_target="tpu_custom_call" | custom-call | flops 5637144576 | bytes 16777216 | tf_op jit(solution)/shard_map/pallas_call | solution.py:178
  101.7 0.0 copy-start
  101.7 3.8 %fusion.28 = (bf16[1,8,2,64,1792]{4,3,2,1,0:T(8,128)(2,1)S(1)}, bf16[1,8,2,64,1792]{4,3,2,1,0:T(8,128)(2,1)S(1)}) fusion(bf16[2,8,2,64,1792]{4,3,2,1,0:T(8,128)(2,1)} %shard_map.76), kind=kLoop, calls=%fused_computation.35 | loop fusion | bytes 14680064 | tf_op jit(solution)/shard_map/slice | solution.py:233
  105.5 0.0 copy-done
  105.5 2.2 %fusion.1 = bf16[1,512,1792]{2,1,0:T(8,128)(2,1)S(1)} fusion(bf16[1024,1792]{1,0:T(8,128)(2,1)S(1)} %bitcast.47, bf16[2,1024,512]{2,1,0:T(8,128)(2,1)S(1)} %copy-done), kind=kOutput, calls=%fused_computation.10 | convolution fusion | flops 1879965696 | bytes 6553600 | tf_op jit(solution)/shard_map/tf,td->fd/dot_general | solution.py:224
  107.7 0.0 slice-start
  107.7 2.2 %fusion.3 = bf16[1,512,1792]{2,1,0:T(8,128)(2,1)S(1)} fusion(bf16[1024,1792]{1,0:T(8,128)(2,1)S(1)} %bitcast.49, bf16[2,1024,512]{2,1,0:T(8,128)(2,1)S(1)} %copy-done), kind=kOutput, calls=%fused_computation.12 | convolution fusion | flops 1879965696 | bytes 6553600 | tf_op jit(solution)/shard_map/tf,td->fd/dot_general | solution.py:224
  109.9 0.0 slice-start.1
  109.9 2.2 %fusion.2 = bf16[1,512,1792]{2,1,0:T(8,128)(2,1)S(1)} fusion(bf16[1024,1792]{1,0:T(8,128)(2,1)S(1)} %bitcast.50, bf16[2,1024,512]{2,1,0:T(8,128)(2,1)S(1)} %copy-done), kind=kOutput, calls=%fused_computation.11 | convolution fusion | flops 1879965696 | bytes 6553600 | tf_op jit(solution)/shard_map/tf,td->fd/dot_general | solution.py:224
  112.1 3.0 %pad_maximum_fusion = bf16[3,512,1792]{2,1,0:T(8,128)(2,1)} fusion(bf16[1,512,1792]{2,1,0:T(8,128)(2,1)S(1)} %fusion.3, bf16[1,512,1792]{2,1,0:T(8,128)(2,1)S(1)} %fusion.2, bf16[1,512,1792]{2,1,0:T(8,128)(2,1)S(1)} %fusion.1), kind=kLoop, calls=%fused_computation | loop fusion | flops 5505024 | bytes 11010048 | tf_op jit(solution)/shard_map/stack | solution.py:228
  115.1 0.0 slice-done
  115.1 0.0 slice-done.1
  115.1 2.1 %fusion.18 = f32[1,1024,512]{2,1,0:T(8,128)S(1)} fusion(bf16[1024,1792]{1,0:T(8,128)(2,1)S(1)} %bitcast.51, bf16[3,512,1792]{2,1,0:T(8,128)(2,1)S(1)} %bitcast.46), kind=kOutput, calls=%fused_computation.27 | convolution fusion | flops 1879048192 | bytes 7602176 | tf_op jit(solution)/shard_map/td,fd->tf/dot_general | solution.py:231
  117.2 2.1 %fusion.11 = f32[1024,512]{1,0:T(8,128)S(1)} fusion(bf16[1024,1792]{1,0:T(8,128)(2,1)S(1)} %bitcast.52, bf16[3,512,1792]{2,1,0:T(8,128)(2,1)S(1)} %bitcast.46), kind=kOutput, calls=%fused_computation.20 | convolution fusion | flops 1879048192 | bytes 7602176 | tf_op jit(solution)/shard_map/td,fd->tf/dot_general | solution.py:238
  119.3 2.1 %add_bitcast_fusion = f32[1,1024,512]{2,1,0:T(8,128)S(1)} fusion(f32[1024,512]{1,0:T(8,128)S(1)} %fusion.11, bf16[1024,1792]{1,0:T(8,128)(2,1)S(1)} %bitcast.48, bf16[3,512,1792]{2,1,0:T(8,128)(2,1)S(1)} %bitcast.46), kind=kOutput, calls=%fused_computation.16 | convolution fusion | flops 1879572480 | bytes 9699328 | tf_op jit(solution)/shard_map/td,fd->tf/dot_general | solution.py:231
  121.4 1.3 fusion.4
  122.7 8.8 %fusion = bf16[2,1792,512]{1,2,0:T(8,128)(2,1)} fusion(bf16[2,1024,1792]{2,1,0:T(8,128)(2,1)} %param.5, f32[1,1024,512]{2,1,0:T(8,128)S(1)} %fusion.18, f32[1,1024,512]{2,1,0:T(8,128)S(1)} %add_bitcast_fusion, u8[1024,512]{1,0:T(8,128)(4,1)S(1)} %fusion.23), kind=kOutput, calls=%fused_computation.6 | convolution fusion | flops 3769368576 | bytes 15728640 | tf_op jit(solution)/shard_map/ltd,ltf->ldf/dot_general | solution.py:249
  131.5 5.9 %copy.9 = bf16[2,1792,512]{2,1,0:T(8,128)(2,1)} copy(bf16[2,1792,512]{1,2,0:T(8,128)(2,1)} %fusion) | data formatting | bytes 7340032
  (1 shorter events, 0.0 us)
Async XLA Ops:
  0.6 9.5 %copy-start.1 = (f32[2,512]{1,0:T(2,128)S(1)}, f32[2,512]{1,0:T(2,128)}, u32[]{:S(2)}) copy-start(f32[2,512]{1,0:T(2,128)} %param.8) | copy-start | bytes 12292
  101.7 3.8 %copy-start = (bf16[2,1024,512]{2,1,0:T(8,128)(2,1)S(1)}, bf16[2,1024,512]{2,1,0:T(8,128)(2,1)}, u32[]{:S(2)}) copy-start(bf16[2,1024,512]{2,1,0:T(8,128)(2,1)} %get-tuple-element.8.act_ref) | copy-start | bytes 6291460
  107.7 7.5 %slice-start = ((s8[5505024]{0:T(1024)(128)(4,1)}), s8[4194304]{0:T(1024)(128)(4,1)S(1)}, s32[]{:S(2)}) async-start(s8[5505024]{0:T(1024)(128)(4,1)} %bitcast.45), calls=%async_computation | async-start | bytes 8388608
  109.9 5.2 %slice-start.1 = ((s8[5505024]{0:T(1024)(128)(4,1)}), s8[1310720]{0:T(1024)(128)(4,1)S(1)}, s32[]{:S(2)}) async-start(s8[5505024]{0:T(1024)(128)(4,1)} %bitcast.45), calls=%async_computation.1 | async-start | bytes 2621440

commit v2 on v1

v2 whole, which is shorter than its diff:
```python
import functools

import jax
import jax.numpy as jnp
from jax import lax
from jax.experimental import pallas as pl
from jax.experimental.pallas import tpu as pltpu
from jax.sharding import PartitionSpec as P

MESH = pl.DeviceIdType.MESH


def pair_index(source, target):
    return target * (target + 1) // 2 + source


def ring_place(index, ring, folded):
    if not folded:
        return index
    side, along = index % 2, index // 2
    return (1 - side) * along + side * (ring - 1 - along)


def ring_index(place, ring, folded):
    if not folded:
        return place
    side = place // (ring // 2)
    return (1 - side) * (2 * place) + side * (2 * (ring - 1 - place) + 1)


def step_kernel(
    ring, folded, scale,
    resid_hbm, enc_hbm, bias_ref, dec_hbm, target_hbm,
    act_hbm, err_hbm, grad_hbm, bias_grad,
    resid, enc, dec, act, mask, err, grad,
    own_part, pair_send, pair_recv, run_send, run_recv, target_own,
    load_sems, resid_sems, store_sems, pair_sems, run_sems, gather_sems, share_sems,
):
    layers, _, cores, rows, width = err.shape
    half = ring // 2
    core = lax.axis_index("latent")
    other = 1 - core
    me = ring_place(lax.axis_index("layer"), ring, folded)

    def place(distance):
        return (me + distance + ring) % ring

    def in_order(order):
        return place((half - (order + 1) // 2) * (2 * (order % 2) - 1))

    neighbour = {step: {"layer": ring_index(place(step), ring, folded)} for step in (1, -1)}
    sibling = {"latent": other}

    def resid_load(q):
        return pltpu.make_async_copy(resid_hbm.at[:, q], resid.at[:, q], resid_sems.at[q])

    enc_load = pltpu.make_async_copy(enc_hbm, enc, load_sems.at[0])
    dec_load = pltpu.make_async_copy(dec_hbm, dec, load_sems.at[1])
    target_load = pltpu.make_async_copy(
        target_hbm.at[:, me, core], target_own, load_sems.at[2]
    )
    enc_load.start()
    for order in range(3):
        resid_load(in_order(order)).start()
    dec_load.start()
    for order in range(3, ring):
        resid_load(in_order(order)).start()
    target_load.start()

    barrier = pltpu.get_barrier_semaphore()
    for device in (neighbour[1], neighbour[-1], sibling):
        pl.semaphore_signal(barrier, inc=1, device_id=device, device_id_type=MESH)
    pl.semaphore_wait(barrier, 3)

    chains = [(0, 1, half), (1, -1, half), (0, -1, half - 1), (1, 1, half - 1)]

    def pair_copy(q):
        return pltpu.make_async_remote_copy(
            src_ref=pair_send.at[:, q], dst_ref=pair_recv.at[:, q],
            send_sem=pair_sems.at[0, q], recv_sem=pair_sems.at[1, q],
            device_id=sibling, device_id_type=MESH,
        )

    def run_copy(chain, step):
        return pltpu.make_async_remote_copy(
            src_ref=run_send.at[chain, step], dst_ref=run_recv.at[chain, step],
            send_sem=run_sems.at[0, chain, step], recv_sem=run_sems.at[1, chain, step],
            device_id=neighbour[chains[chain][1]], device_id_type=MESH,
        )

    def gather_copy(chain, step):
        layer, direction, _ = chains[chain]
        block = err.at[layer, place(-direction * step), core]
        return pltpu.make_async_remote_copy(
            src_ref=block, dst_ref=block,
            send_sem=gather_sems.at[0, chain, step], recv_sem=gather_sems.at[1, chain, step],
            device_id=neighbour[direction], device_id_type=MESH,
        )

    def share_copy(layer, q, sender):
        block = err.at[layer, q, sender]
        return pltpu.make_async_remote_copy(
            src_ref=block, dst_ref=block,
            send_sem=share_sems.at[0, layer, q], recv_sem=share_sems.at[1, layer, q],
            device_id=sibling, device_id_type=MESH,
        )

    kept = ((act, act_hbm), (err, err_hbm), (grad, grad_hbm))

    def store(i, q):
        here, there = kept[i]
        return pltpu.make_async_copy(here.at[:, q], there.at[:, q], store_sems.at[i, q])

    def encode(order, carry):
        q = in_order(order)
        resid_load(q).wait()
        for layer in range(layers):
            pre = jnp.dot(
                resid[layer, q], enc[layer], preferred_element_type=jnp.float32
            ) + bias_ref[layer]
            act[layer, q] = jnp.maximum(pre, 0.0).astype(jnp.bfloat16)
            mask[layer, q] = jnp.where(pre > 0.0, 1.0, 0.0).astype(jnp.bfloat16)
        store(0, q).start()
        return carry

    def decode(order, carry):
        q = in_order(order)
        for target in range(layers):
            total = jnp.dot(
                act[0, q], dec[pair_index(0, target)], preferred_element_type=jnp.float32
            )
            for source in range(1, target + 1):
                total = total + jnp.dot(
                    act[source, q], dec[pair_index(source, target)],
                    preferred_element_type=jnp.float32,
                )
            own_part[target, q] = jnp.where(core == 0, total[:rows], total[rows:])
            pair_send[target, q] = jnp.where(core == 0, total[rows:], total[:rows]).astype(
                jnp.bfloat16
            )
        pair_copy(q).start()
        return carry

    def own_sum(layer, q):
        return own_part[layer, q] + pair_recv[layer, q].astype(jnp.float32)

    def backward(q):
        for layer in range(layers):
            share_copy(layer, q, other).wait_recv()
        store(1, q).start()
        for source in range(layers):
            total = jnp.zeros((cores * rows, act.shape[3]), jnp.float32)
            for target in range(source, layers):
                total = total + lax.dot_general(
                    err[target, q].reshape(cores * rows, width),
                    dec[pair_index(source, target)],
                    (((1,), (1,)), ((), ())), preferred_element_type=jnp.float32,
                )
            value = jnp.where(mask[source, q].astype(jnp.float32) > 0.0, total, 0.0)
            bias_grad[source] += jnp.sum(value, axis=0, keepdims=True)
            grad[source, q] = value.astype(jnp.bfloat16)
        store(2, q).start()

    enc_load.wait()
    lax.fori_loop(0, 3, encode, 0)
    dec_load.wait()
    lax.fori_loop(0, 3, decode, 0)
    for step in range(half):
        for away in {0: (half, half - 1, 1 - half)}.get(
            step, (half - 1 - step, step + 1 - half) if step < half - 1 else (0,)
        ):
            pair_copy(place(away)).wait_recv()
        for chain, (layer, direction, hops) in enumerate(chains):
            if step >= hops:
                continue
            value = own_sum(layer, place(direction * (hops - step)))
            if step > 0:
                run_copy(chain, step - 1).wait_recv()
                value = value + run_recv[chain, step - 1].astype(jnp.float32)
            run_send[chain, step] = value.astype(jnp.bfloat16)
            run_copy(chain, step).start()
        first, last = 2 * step + 3, min(2 * step + 5, ring)
        if first < last:
            lax.fori_loop(first, last, lambda j, c: decode(j, encode(j, c)), 0)

    target_load.wait()
    bias_grad[...] = jnp.zeros_like(bias_grad)
    for layer in range(layers):
        value = own_sum(layer, me)
        for chain, (of, direction, hops) in sorted(
            enumerate(chains), key=lambda item: item[1][2]
        ):
            if of == layer:
                run_copy(chain, hops - 1).wait_recv()
                value = value + run_recv[chain, hops - 1].astype(jnp.float32)
        error = (value - target_own[layer].astype(jnp.float32)) * scale
        err[layer, me, core] = error.astype(jnp.bfloat16)
        for chain, (of, direction, hops) in enumerate(chains):
            if of == layer:
                gather_copy(chain, 0).start()
        share_copy(layer, me, core).start()

    backward(me)
    for step in range(half):
        for chain, (layer, direction, hops) in enumerate(chains):
            if step >= hops:
                continue
            gather_copy(chain, step).wait_recv()
            if step + 1 < hops:
                gather_copy(chain, step + 1).start()
            share_copy(layer, place(-direction * (step + 1)), core).start()

        def both_sides(side, carry, away=step + 1):
            backward(place(away * (1 - 2 * side)))
            return carry

        lax.fori_loop(0, 2 if step + 1 < half else 1, both_sides, 0)

    for chain, (layer, direction, hops) in enumerate(chains):
        for step in range(hops):
            run_copy(chain, step).wait_send()
            gather_copy(chain, step).wait_send()

    def finish(q, carry):
        pair_copy(q).wait_send()
        for layer in range(layers):
            share_copy(layer, q, core).wait_send()
        for i in range(len(kept)):
            store(i, q).wait()
        return carry

    lax.fori_loop(0, ring, finish, 0)


def step(residual_in, mlp_target, enc_weight, enc_bias, dec_weight, ring, cores, scale):
    layers, tokens, width = mlp_target.shape
    features = enc_weight.shape[2]
    rows = tokens // (ring * cores)
    half = ring // 2
    halves = (layers, ring, cores, rows, width)
    by_width = (layers, ring, cores * rows, width)
    by_feature = (layers, ring, cores * rows, features)
    anywhere = pl.BlockSpec(memory_space=pl.ANY)
    in_vmem = pl.BlockSpec(memory_space=pltpu.VMEM)
    bf16 = jnp.bfloat16
    act, err, grad, bias_grad = pl.pallas_call(
        functools.partial(step_kernel, ring, ring == 8, scale),
        out_shape=(
            jax.ShapeDtypeStruct(by_feature, bf16),
            jax.ShapeDtypeStruct(halves, bf16),
            jax.ShapeDtypeStruct(by_feature, bf16),
            jax.ShapeDtypeStruct((layers, 1, features), jnp.float32),
        ),
        in_specs=[anywhere, anywhere, in_vmem, anywhere, anywhere],
        out_specs=(anywhere, anywhere, anywhere, in_vmem),
        scratch_shapes=[
            pltpu.VMEM(by_width, bf16),
            pltpu.VMEM(enc_weight.shape, bf16),
            pltpu.VMEM(dec_weight.shape, bf16),
            pltpu.VMEM(by_feature, bf16),
            pltpu.VMEM(by_feature, bf16),
            pltpu.VMEM(halves, bf16),
            pltpu.VMEM(by_feature, bf16),
            pltpu.VMEM((layers, ring, rows, width), jnp.float32),
            pltpu.VMEM((layers, ring, rows, width), bf16),
            pltpu.VMEM((layers, ring, rows, width), bf16),
            pltpu.VMEM((4, half, rows, width), bf16),
            pltpu.VMEM((4, half, rows, width), bf16),
            pltpu.VMEM((layers, rows, width), bf16),
            pltpu.SemaphoreType.DMA((3,)),
            pltpu.SemaphoreType.DMA((ring,)),
            pltpu.SemaphoreType.DMA((3, ring)),
            pltpu.SemaphoreType.DMA((2, ring)),
            pltpu.SemaphoreType.DMA((2, 4, half)),
            pltpu.SemaphoreType.DMA((2, 4, half)),
            pltpu.SemaphoreType.DMA((2, layers, ring)),
        ],
        compiler_params=pltpu.CompilerParams(
            collective_id=0, has_side_effects=True, vmem_limit_bytes=60 * 1024 * 1024
        ),
        cost_estimate=pl.CostEstimate(
            flops=16 * tokens * width * features, bytes_accessed=2 ** 25, transcendentals=0
        ),
    )(
        residual_in.reshape(by_width), enc_weight, enc_bias.reshape(layers, 1, features),
        dec_weight, mlp_target.reshape(halves),
    )
    return (
        act.reshape(layers, tokens, features),
        err.reshape(layers, tokens, width),
        grad.reshape(layers, tokens, features),
        bias_grad.reshape(layers, features),
    )


def token_sum_kernel(left_ref, right_ref, out_ref):
    out_ref[0] = lax.dot_general(
        left_ref[0], right_ref[0], (((0,), (0,)), ((), ())),
        preferred_element_type=jnp.float32,
    ).astype(out_ref.dtype)


def token_sum(left, right, pairs, left_of, right_of, cuts):
    _, tokens, rows = left.shape
    width = right.shape[2]
    return pl.pallas_call(
        token_sum_kernel,
        out_shape=jax.ShapeDtypeStruct((pairs, rows, width), jnp.bfloat16),
        grid=(pairs, cuts),
        in_specs=[
            pl.BlockSpec((1, tokens, rows // cuts), lambda p, i: (left_of(p), 0, i)),
            pl.BlockSpec((1, tokens, width), lambda p, i: (right_of(p), 0, 0)),
        ],
        out_specs=pl.BlockSpec((1, rows // cuts, width), lambda p, i: (p, i, 0)),
        compiler_params=pltpu.CompilerParams(vmem_limit_bytes=56 * 1024 * 1024),
        cost_estimate=pl.CostEstimate(
            flops=2 * pairs * tokens * rows * width,
            bytes_accessed=2 * pairs * (tokens * (rows + width) + rows * width),
            transcendentals=0,
        ),
    )(left, right)


def body(ring, cores, residual_in, mlp_target, enc_weight, enc_bias, dec_weight):
    layers, tokens, _ = residual_in.shape
    assert layers == 2 and cores == 2
    act, err, grad, grad_bias = step(
        residual_in, mlp_target, enc_weight, enc_bias, dec_weight,
        ring, cores, float(tokens) ** (-0.5),
    )
    grad_dec = token_sum(act, err, 3, lambda p: p // 2, lambda p: (p + 1) // 2, 1)
    grad_encoder = token_sum(residual_in, grad, 2, lambda p: p, lambda p: p, 2)
    return (grad_encoder, grad_bias, grad_dec)


def solution(mesh):
    placed = (
        P(None, "group", None),
        P(None, "group", None),
        P(None, None, ("layer", "latent")),
        P(None, ("layer", "latent")),
        P(None, ("layer", "latent"), None),
    )
    return jax.shard_map(
        functools.partial(body, mesh.shape["layer"], mesh.shape["latent"]),
        mesh=mesh,
        in_specs=placed,
        out_specs=(
            P("group", None, ("layer", "latent")),
            P("group", ("layer", "latent")),
            P("group", ("layer", "latent"), None),
        ),
        check_vma=False,
    )
```

time: 138 us -> 116 us (0.84)
  matrix products: 31.1 us -> 0 us
  Pallas kernels: 90.8 us -> 113 us
  local copies, waits for them, and re-layouts: 9.73 us -> 1.88 us
  other arithmetic: 5.09 us -> 0 us
    dot_general x8 -> x0, matrix products: 31.1 us -> none  [the longest x1 9.5 us: body(): jnp.einsum('ltd,ldf->ltf', residual_in, enc_weight, preferred_element_typ...]
    pallas_call x1 -> x3, Pallas kernels: 90.8 us -> 113 us  [the longest x1 94.3 us: step(): pl.pallas_call(functools.partial(step_kernel, ring, ring == 8, scale), ou...]
    unnamed x9 -> x3, local copies, waits for them, and re-layouts: 5.97 us -> 0.6 us
    slice x1 -> x0, local copies, waits for them, and re-layouts: 3.76 us -> none  [body(): error_all[source]]
    another operation x1 -> x0, other arithmetic: 3.04 us -> none  [body(): grad_dec = jnp.stack(dec_grads)]
where the time goes in v2:
time: 116 us; the launch traced here: 115 us
  Pallas kernels  113 us (97%)
  local copies, waits for them, and re-layouts  1.88 us (2%)
    pallas_call x1, Pallas kernels, step(): pl.pallas_call(functools.partial(step_kernel, ring, ring == 8, scale), ou...  94.3 us
    pallas_call x2, Pallas kernels, token_sum(): pl.pallas_call(token_sum_kernel, out_shape=jax.ShapeDtypeStruct((pairs, r...  18.4 us

profile of v2, /device:TPU:0, one launch (start us, length us, event | category | flops | bytes accessed | tf_op | source)
XLA Modules:
  0.0 115.3 jit_solution(8054455884953044746)
XLA Ops:
  0.6 1.3 %reshape.28.bias_ref = f32[2,1,512]{2,1,0:T(1,128)} reshape(f32[2,512]{1,0:T(2,128)} %param.8) | data formatting | bytes 8192 | tf_op jit(solution)/shard_map/reshape | solution.py:285
  1.9 94.3 %shard_map.76 = (bf16[2,8,128,512]{3,2,1,0:T(8,128)(2,1)}, bf16[2,8,2,64,1792]{4,3,2,1,0:T(8,128)(2,1)}, bf16[2,8,128,512]{3,2,1,0:T(8,128)(2,1)}, f32[2,1,512]{2,1,0:T(1,128)}) custom-call(bf16[2,8,128,1792]{3,2,1,0:T(8,128)(2,1)} %bitcast.10, bf16[2,1792,512]{2,1,0:T(8,128)(2,1)} %enc_hbm.1, f32[2,1,512]{2,1,0:T(1,128)} %reshape.28.bias_ref, ...), custom_call_target="tpu_custom_call" | custom-call | flops 15032385536 | bytes 33554432 | tf_op jit(solution)/shard_map/pallas_call | solution.py:246
  96.3 10.1 %shard_map.78 = bf16[3,512,1792]{2,1,0:T(8,128)(2,1)} custom-call(bf16[2,1024,512]{2,1,0:T(8,128)(2,1)} %bitcast.13, bf16[2,1024,1792]{2,1,0:T(8,128)(2,1)} %bitcast.11), custom_call_target="tpu_custom_call" | custom-call | flops 5637144576 | bytes 19660800 | tf_op jit(solution)/shard_map/pallas_call | solution.py:306
  106.3 0.0 copy-start
  106.3 8.4 %shard_map.77 = bf16[2,1792,512]{2,1,0:T(8,128)(2,1)} custom-call(bf16[2,1024,1792]{2,1,0:T(8,128)(2,1)} %left_ref.1, bf16[2,1024,512]{2,1,0:T(8,128)(2,1)} %bitcast.12), custom_call_target="tpu_custom_call" | custom-call | flops 3758096384 | bytes 13107200 | tf_op jit(solution)/shard_map/pallas_call | solution.py:306
  114.7 0.0 copy-done
  114.7 0.6 copy.10
Async XLA Ops:
  106.3 8.4 %copy-start = (f32[2,1,512]{2,1,0:T(1,128)S(1)}, f32[2,1,512]{2,1,0:T(1,128)}, u32[]{:S(2)}) copy-start(f32[2,1,512]{2,1,0:T(1,128)} %get-tuple-element.8) | copy-start | bytes 12292

commit v3 on v2

--- a/solution.py
+++ b/solution.py
@@ -117,7 +117,7 @@
         for layer in range(layers):
             pre = jnp.dot(
                 resid[layer, q], enc[layer], preferred_element_type=jnp.float32
-            ) + bias_ref[layer]
+            ) + bias_ref[pl.ds(layer, 1), :]
             act[layer, q] = jnp.maximum(pre, 0.0).astype(jnp.bfloat16)
             mask[layer, q] = jnp.where(pre > 0.0, 1.0, 0.0).astype(jnp.bfloat16)
         store(0, q).start()
@@ -157,22 +157,28 @@
                     (((1,), (1,)), ((), ())), preferred_element_type=jnp.float32,
                 )
             value = jnp.where(mask[source, q].astype(jnp.float32) > 0.0, total, 0.0)
-            bias_grad[source] += jnp.sum(value, axis=0, keepdims=True)
+            bias_grad[pl.ds(source, 1), :] += jnp.sum(value, axis=0, keepdims=True)
             grad[source, q] = value.astype(jnp.bfloat16)
         store(2, q).start()
 
     enc_load.wait()
-    lax.fori_loop(0, 3, encode, 0)
+    encode(0, 0)
     dec_load.wait()
-    lax.fori_loop(0, 3, decode, 0)
+    decode(0, 0)
+    lax.fori_loop(1, 2, lambda j, c: decode(j, encode(j, c)), 0)
     for step in range(half):
-        for away in {0: (half, half - 1, 1 - half)}.get(
-            step, (half - 1 - step, step + 1 - half) if step < half - 1 else (0,)
-        ):
-            pair_copy(place(away)).wait_recv()
+        if step == 0:
+            pair_copy(place(half)).wait_recv()
+        else:
+            for away in (half - 1 - step, step + 1 - half) if step < half - 1 else (0,):
+                pair_copy(place(away)).wait_recv()
         for chain, (layer, direction, hops) in enumerate(chains):
             if step >= hops:
                 continue
+            if step == 0 and chain == 2:
+                lax.fori_loop(2, 3, lambda j, c: decode(j, encode(j, c)), 0)
+                for away in (half - 1, 1 - half):
+                    pair_copy(place(away)).wait_recv()
             value = own_sum(layer, place(direction * (hops - step)))
             if step > 0:
                 run_copy(chain, step - 1).wait_recv()
@@ -249,7 +255,7 @@
             jax.ShapeDtypeStruct(by_feature, bf16),
             jax.ShapeDtypeStruct(halves, bf16),
             jax.ShapeDtypeStruct(by_feature, bf16),
-            jax.ShapeDtypeStruct((layers, 1, features), jnp.float32),
+            jax.ShapeDtypeStruct((layers, features), jnp.float32),
         ),
         in_specs=[anywhere, anywhere, in_vmem, anywhere, anywhere],
         out_specs=(anywhere, anywhere, anywhere, in_vmem),
@@ -282,14 +288,14 @@
             flops=16 * tokens * width * features, bytes_accessed=2 ** 25, transcendentals=0
         ),
     )(
-        residual_in.reshape(by_width), enc_weight, enc_bias.reshape(layers, 1, features),
+        residual_in.reshape(by_width), enc_weight, enc_bias,
         dec_weight, mlp_target.reshape(halves),
     )
     return (
         act.reshape(layers, tokens, features),
         err.reshape(layers, tokens, width),
         grad.reshape(layers, tokens, features),
-        bias_grad.reshape(layers, features),
+        bias_grad,
     )
 
 

time: 116 us -> 110 us (0.948)
  Pallas kernels: 113 us -> 108 us
  local copies, waits for them, and re-layouts: 1.88 us -> 0.6 us
    pallas_call x1, Pallas kernels: 94.3 us -> 90 us  [step(): pl.pallas_call(functools.partial(step_kernel, ring, ring == 8, scale), ou...]
    reshape x1 -> x0, local copies, waits for them, and re-layouts: 1.28 us -> none  [step(): enc_bias.reshape(layers, 1, features)]
where the time goes in v3:
time: 110 us
  Pallas kernels  108 us (98%)
    pallas_call x1, Pallas kernels, step(): pl.pallas_call(functools.partial(step_kernel, ring, ring == 8, scale), ou...  90 us
    pallas_call x2, Pallas kernels, token_sum(): pl.pallas_call(token_sum_kernel, out_shape=jax.ShapeDtypeStruct((pairs, r...  18.4 us

profile of v3, /device:TPU:0, one launch (start us, length us, event | category | flops | bytes accessed | tf_op | source)
XLA Modules:
  0.0 109.6 jit_solution(10809994713255731689)
XLA Ops:
  0.6 90.0 %shard_map.76 = (bf16[2,8,128,512]{3,2,1,0:T(8,128)(2,1)}, bf16[2,8,2,64,1792]{4,3,2,1,0:T(8,128)(2,1)}, bf16[2,8,128,512]{3,2,1,0:T(8,128)(2,1)}, f32[2,512]{1,0:T(2,128)}) custom-call(bf16[2,8,128,1792]{3,2,1,0:T(8,128)(2,1)} %bitcast.6, bf16[2,1792,512]{2,1,0:T(8,128)(2,1)} %enc_hbm.1, f32[2,512]{1,0:T(2,128)} %bias_ref.1, bf16[3,512,1792]{2,1,0:T(8,128)(2,1)} %dec_hbm.1, ...), custom_call_target="tpu_custom_call" | custom-call | flops 15032385536 | bytes 33554432 | tf_op jit(solution)/shard_map/pallas_call | solution.py:252
  90.6 10.1 %shard_map.78 = bf16[3,512,1792]{2,1,0:T(8,128)(2,1)} custom-call(bf16[2,1024,512]{2,1,0:T(8,128)(2,1)} %bitcast.9, bf16[2,1024,1792]{2,1,0:T(8,128)(2,1)} %bitcast.7), custom_call_target="tpu_custom_call" | custom-call | flops 5637144576 | bytes 19660800 | tf_op jit(solution)/shard_map/pallas_call | solution.py:312
  100.7 0.0 copy-start
  100.7 8.4 %shard_map.77 = bf16[2,1792,512]{2,1,0:T(8,128)(2,1)} custom-call(bf16[2,1024,1792]{2,1,0:T(8,128)(2,1)} %left_ref.1, bf16[2,1024,512]{2,1,0:T(8,128)(2,1)} %bitcast.8), custom_call_target="tpu_custom_call" | custom-call | flops 3758096384 | bytes 13107200 | tf_op jit(solution)/shard_map/pallas_call | solution.py:312
  109.0 0.0 copy-done
  109.0 0.6 copy.9
Async XLA Ops:
  100.7 8.4 %copy-start = (f32[2,512]{1,0:T(2,128)S(1)}, f32[2,512]{1,0:T(2,128)}, u32[]{:S(2)}) copy-start(f32[2,512]{1,0:T(2,128)} %get-tuple-element.15) | copy-start | bytes 12292
